TPU v7x, 512 devices: a whole 4x4x16 slice. The times are simulated.
512 devices in a mesh: row: 128 (over x, z, y_hi), ch: 4 (over y_lo, core).
Axes of the slice: x: 4, y: 4 (y_hi: 2, y_lo: 2; y = y_hi * 2 + y_lo), z: 16, core: 2. Of those that a mesh axis runs over, the one named last changes fastest.
Arguments:
- pair_rep: bfloat16 [128, 128, 128], P('ch', 'row'), may hold values from -6 to 6
- residue_mask: int32 [128], replicated, may hold values 0 or 1
- chain_ids: int32 [128], replicated, may hold values from 0 to 3, never falling along the last dimension, each value on 1 to 64 neighbouring positions
- in_gain: float32 [2, 128], replicated, may hold values from 0.5 to 1.5
- in_bias: float32 [2, 128], replicated, may hold values from -3 to 3
- w_proj: bfloat16 [2, 128, 4, 128], P(None, None, None, 'ch'), may hold values from -0.5 to 0.5
- w_gate: bfloat16 [2, 128, 128], P(None, None, 'ch'), may hold values from -0.5 to 0.5
- pair_bias: float32 [2, 128], P(None, 'ch'), may hold values from -4 to 4
- out_gain: float32 [2, 128], P(None, 'ch'), may hold values from 0.5 to 1.5
- out_bias: float32 [2, 128], P(None, 'ch'), may hold values from -3 to 3
- w_out: bfloat16 [2, 128, 128], P(None, 'ch'), may hold values from -0.5 to 0.5
Outputs:
- pair_out: bfloat16 [128, 128, 128], P('ch', 'row')
Inputs may be any that keep to these rules, and one draw needn't show every extreme that they name: `chain_ids`: chain numbers never fall along the residues; each chain has 1 to 64 residues.
All inputs are finite; a program needn't handle non-finite values.
Results may differ from a plain program's by a relative error of at most 0.013.
Values may be sent and summed in bfloat16 or wider, within the bound.
No kernel may reach another device: no remote copies, remote signals or barrier semaphores. Data moves between devices by JAX's collectives and lax.ppermute only.
A program may use at most 64 MiB of HBM per device.

v0:
```python
import jax
import jax.numpy as jnp
from jax import lax
from jax.sharding import PartitionSpec as P

epsilon = 1e-05


def in_order(tiles, dim):
    tiles = jnp.moveaxis(tiles, 0, dim)
    dims = tiles.shape
    return tiles.reshape(*dims[:dim], dims[dim] * dims[dim + 1], *dims[dim + 2 :])


def from_everyone(x, axis):
    devices = lax.axis_size(axis)
    return lax.all_to_all(jnp.broadcast_to(x[None], (devices, *x.shape)), axis, 0, 0, tiled=True)


def gathered_copies(x, axis, dim):
    return in_order(from_everyone(x, axis), dim)


def of_everyone(x, axis):
    return from_everyone(x, axis).sum(axis=0)


def together(arrays, axis):
    ends = [0]
    for a in arrays:
        ends.append(ends[-1] + a.size)
    so_far = of_everyone(jnp.concatenate([a.ravel() for a in arrays]), axis)
    return tuple((so_far[b:e].reshape(a.shape) for a, b, e in zip(arrays, ends, ends[1:])))


def in_blocks(x, dim, devices):
    before, after = (x.shape[:dim], x.shape[dim + 1 :])
    return jnp.moveaxis(x.reshape(*before, devices, -1, *after), dim, 0)


def sum_at_owner(x, axis, dim):
    devices = lax.axis_size(axis)
    tiles = lax.all_to_all(in_blocks(x, dim, devices), axis, 0, 0, tiled=True)
    return jnp.sum(tiles.astype(jnp.float32), axis=0)


def sent_together(arrays, axis, split_dim, concat_dim, along):
    widths = [a.shape[along] for a in arrays]
    both = jnp.concatenate(arrays, axis=along)
    result = lax.all_to_all(both, axis, split_axis=split_dim, concat_axis=concat_dim, tiled=True)
    return tuple(jnp.split(result, [sum(widths[:k]) for k in range(1, len(widths))], axis=along))


def channel_norm(values, norm_gain, norm_bias):
    mean_val = jnp.mean(values, axis=0)
    variance = jnp.mean(values * values, axis=0) - mean_val * mean_val
    return (values - mean_val) * lax.rsqrt(variance + epsilon) * norm_gain[
        :, None, None
    ] + norm_bias[:, None, None]


def prepare(
    pair_local, layer, in_gain, in_bias, w_proj, w_gate, pair_bias, mask_rows, mask_cols, same_chain
):
    full_pair = gathered_copies(pair_local, "ch", 0)
    normed = channel_norm(full_pair.astype(jnp.float32), in_gain[layer], in_bias[layer]).astype(
        jnp.bfloat16
    )
    projected = jnp.einsum(
        "cij,cpd->pdij", normed, w_proj[layer], preferred_element_type=jnp.float32
    )
    pair_mask = mask_rows[:, None] * mask_cols[None, :]
    first_arm = (jax.nn.sigmoid(projected[0]) * projected[1] * pair_mask).astype(jnp.bfloat16)
    second_arm = (jax.nn.sigmoid(projected[2]) * projected[3] * pair_mask).astype(jnp.bfloat16)
    logits = jnp.einsum("cij,cd->dij", normed, w_gate[layer], preferred_element_type=jnp.float32)
    logits = logits + pair_bias[layer][:, None, None] * same_chain[None]
    return (first_arm, second_arm, jax.nn.sigmoid(logits))


def finish(product_sum, gating, layer, out_gain, out_bias, w_out):
    totals = together(
        (jnp.sum(product_sum, axis=0), jnp.sum(product_sum * product_sum, axis=0)), "ch"
    )
    channels = product_sum.shape[0] * lax.axis_size("ch")
    mean_val = totals[0] / channels
    variance = totals[1] / channels - mean_val * mean_val
    scaled = (product_sum - mean_val) * lax.rsqrt(variance + epsilon)
    normed = (scaled * out_gain[layer][:, None, None] + out_bias[layer][:, None, None]).astype(
        jnp.bfloat16
    )
    columns = w_out[layer]
    mixed = sum_at_owner(
        jnp.einsum("dij,dc->cij", normed, columns, preferred_element_type=jnp.float32).astype(
            jnp.bfloat16
        ),
        "ch",
        0,
    )
    return gating * mixed


def to_owner(first_arm, second_arm):
    first_quarter, second_quarter = sent_together((first_arm, second_arm), "ch", 2, 0, 1)
    return sent_together((first_quarter, second_quarter), "row", 0, 1, 2)


def to_rows(owned):
    blocks = lax.all_to_all(owned, "row", split_axis=1, concat_axis=0, tiled=True)
    return lax.all_to_all(blocks, "ch", split_axis=0, concat_axis=2, tiled=True)


def body(
    pair_rep,
    residue_mask,
    chain_ids,
    in_gain,
    in_bias,
    w_proj,
    w_gate,
    pair_bias,
    out_gain,
    out_bias,
    w_out,
):
    rows_here = pair_rep.shape[1]
    row_start = lax.axis_index("row") * rows_here
    mask_cols = residue_mask.astype(jnp.float32)
    mask_rows = lax.dynamic_slice_in_dim(mask_cols, row_start, rows_here)
    chain_rows = lax.dynamic_slice_in_dim(chain_ids, row_start, rows_here)
    same_chain = (chain_rows[:, None] == chain_ids[None, :]).astype(jnp.float32)
    first_arm, second_arm, gating = prepare(
        pair_rep, 0, in_gain, in_bias, w_proj, w_gate, pair_bias, mask_rows, mask_cols, same_chain
    )
    first_own, second_own = to_owner(first_arm, second_arm)
    partial_sum = jnp.einsum(
        "dik,djk->dij", first_own, second_own, preferred_element_type=jnp.float32
    )
    owned_sum = sum_at_owner(partial_sum.astype(jnp.bfloat16), "ch", 2)
    product_sum = to_rows(owned_sum)
    middle = (
        pair_rep.astype(jnp.float32) + finish(product_sum, gating, 0, out_gain, out_bias, w_out)
    ).astype(jnp.bfloat16)
    in_first, in_second, in_gating = prepare(
        middle, 1, in_gain, in_bias, w_proj, w_gate, pair_bias, mask_rows, mask_cols, same_chain
    )
    left_own, right_own = to_owner(in_first, in_second)
    owned_product = jnp.einsum(
        "dki,dkj->dij",
        gathered_copies(left_own, "ch", 2),
        right_own,
        preferred_element_type=jnp.float32,
    )
    in_product = to_rows(owned_product)
    update = finish(in_product, in_gating, 1, out_gain, out_bias, w_out)
    return (middle.astype(jnp.float32) + update).astype(jnp.bfloat16)


def solution(mesh):
    return jax.shard_map(
        body,
        mesh=mesh,
        in_specs=(
            P("ch", "row", None),
            P(),
            P(),
            P(),
            P(),
            P(None, None, None, "ch"),
            P(None, None, "ch"),
            P(None, "ch"),
            P(None, "ch"),
            P(None, "ch"),
            P(None, "ch", None),
        ),
        out_specs=P("ch", "row", None),
        check_vma=False,
    )
```

profile of v0, /device:TPU:1, one launch (start us, length us, event | category | flops | bytes accessed | tf_op | source)
XLA Modules:
  0.0 200.2 jit_solution(12180103836867893405)
XLA Ops:
  0.0 1.3 broadcast_in_dim.17
  1.3 10.1 %all-to-all-start = ((bf16[4,32,1,128]{3,1,2,0:T(8,128)(2,1)}), bf16[4,32,1,128]{3,1,2,0:T(8,128)(2,1)S(1)}, u32[]{:S(2)}, u32[]{:S(2)}) async-start(bf16[4,32,1,128]{3,1,2,0:T(8,128)(2,1)} %broadcast_in_dim.17), calls=%async_computation | async-start | bytes 65536 | tf_op jit(solution)/shard_map/all_to_all | solution.py:17
  11.5 0.7 copy-done.9
  12.1 0.7 copy-done.3
  12.8 0.6 dynamic_slice.7
  13.4 0.6 broadcast_multiply_fusion
  14.1 0.6 all-to-all-done
  14.7 0.2 fusion.70
  14.9 0.1 copy.81
  15.1 0.1 reshape.1148
  15.2 6.2 %all_to_all.162 = bf16[4,2,1024]{2,1,0:T(2,128)(2,1)S(1)} all-to-all(bf16[4,2,1024]{2,1,0:T(2,128)(2,1)S(1)} %reshape.1148), channel_id=1, replica_groups=mesh['row'=128,'ch'=4] {'ch'}, dimensions={0} | all-to-all | bytes 32768 | tf_op jit(solution)/shard_map/all_to_all | solution.py:50
  21.4 0.1 reshape.1149
  21.6 0.1 all_to_all.118
  21.7 0.1 copy.83
  21.9 32.3 %all_to_all.163 = bf16[128,1,64]{2,1,0:T(2,128)(2,1)S(1)} all-to-all(bf16[128,1,64]{2,1,0:T(2,128)(2,1)S(1)} %copy.83), channel_id=1, replica_groups=mesh['row'=128,'ch'=4] {'row'}, dimensions={0} | all-to-all | bytes 32768 | tf_op jit(solution)/shard_map/all_to_all | solution.py:50
  54.3 0.2 convolution_convert_fusion.2
  54.5 7.7 %all_to_all.164 = bf16[4,1,128,32]{2,3,1,0:T(8,128)(2,1)S(1)} all-to-all(bf16[4,1,128,32]{2,3,1,0:T(8,128)(2,1)S(1)} %bitcast.246), channel_id=1, replica_groups=mesh['row'=128,'ch'=4] {'ch'}, dimensions={0} | all-to-all | bytes 65536 | tf_op jit(solution)/shard_map/all_to_all | solution.py:43
  62.2 0.1 copy.86
  62.3 21.3 %all_to_all.165 = f32[1,128,32]{2,0,1:T(1,128)S(1)} all-to-all(f32[1,128,32]{2,0,1:T(1,128)S(1)} %copy.86), channel_id=1, replica_groups=mesh['row'=128,'ch'=4] {'row'}, dimensions={1} | all-to-all | bytes 32768 | tf_op jit(solution)/shard_map/all_to_all | solution.py:108
  83.6 0.5 broadcast.547
  84.1 0.8 reduce.21
  84.9 0.7 reshape.1150
  85.6 5.5 %all-to-all-start.5 = ((f32[4,1,1024]{2,1,0:T(1,128)}), f32[4,1,1024]{2,1,0:T(1,128)S(1)}, u32[]{:S(2)}, u32[]{:S(2)}) async-start(f32[4,1,1024]{2,1,0:T(1,128)} %reshape.1150), calls=%async_computation.5 | async-start | bytes 32768 | tf_op jit(solution)/shard_map/all_to_all | solution.py:109
  91.1 3.1 %all-to-all-done.5 = f32[4,1,1024]{2,1,0:T(1,128)S(1)} async-done(((f32[4,1,1024]{2,1,0:T(1,128)}), f32[4,1,1024]{2,1,0:T(1,128)S(1)}, u32[]{:S(2)}, u32[]{:S(2)}) %all-to-all-start.5) | async-done | bytes 16416 | tf_op jit(solution)/shard_map/all_to_all | solution.py:109
  94.2 0.7 reduce.22
  94.9 0.1 reshape.1151
  95.0 0.1 copy.104
  95.1 0.1 bitcast_reduce_fusion
  95.6 0.6 broadcast_in_dim.18
  96.2 4.1 %all-to-all-start.6 = ((f32[4,1,256]{2,1,0:T(1,128)}), f32[4,1,256]{2,1,0:T(1,128)S(1)}, u32[]{:S(2)}, u32[]{:S(2)}) async-start(f32[4,1,256]{2,1,0:T(1,128)} %broadcast_in_dim.18), calls=%async_computation.6 | async-start | bytes 8192 | tf_op jit(solution)/shard_map/all_to_all | solution.py:17
  100.3 0.6 copy-done.10
  101.0 0.6 dynamic_slice.6
  101.6 0.1 copy.89
  101.7 0.1 all_to_all.127
  101.8 1.6 all-to-all-done.6
  103.4 0.8 convolution_convert_fusion.1
  104.3 3.9 %all-to-all-start.7 = ((bf16[4,32,1,128]{3,1,2,0:T(8,128)(2,1)}), bf16[4,32,1,128]{3,1,2,0:T(8,128)(2,1)S(1)}, u32[]{:S(2)}, u32[]{:S(2)}) async-start(bf16[4,32,1,128]{3,1,2,0:T(8,128)(2,1)} %bitcast.36), calls=%async_computation.7 | async-start | bytes 65536 | tf_op jit(solution)/shard_map/all_to_all | solution.py:43
  108.2 0.6 compare_convert_fusion
  108.9 2.5 %all-to-all-done.7 = bf16[4,32,1,128]{3,1,2,0:T(8,128)(2,1)S(1)} async-done(((bf16[4,32,1,128]{3,1,2,0:T(8,128)(2,1)}), bf16[4,32,1,128]{3,1,2,0:T(8,128)(2,1)S(1)}, u32[]{:S(2)}, u32[]{:S(2)}) %all-to-all-start.7) | async-done | bytes 32800 | tf_op jit(solution)/shard_map/all_to_all | solution.py:43
  111.4 0.2 fusion.17
  111.7 6.3 %all_to_all.166 = bf16[4,32,1,128]{3,1,2,0:T(8,128)(2,1)S(1)} all-to-all(bf16[4,32,1,128]{3,1,2,0:T(8,128)(2,1)S(1)} %broadcast_in_dim.20), channel_id=1, replica_groups=mesh['row'=128,'ch'=4] {'ch'}, dimensions={0} | all-to-all | bytes 65536 | tf_op jit(solution)/shard_map/all_to_all | solution.py:17
  118.0 0.2 fusion.67
  118.3 0.1 copy.94
  118.4 0.1 reshape.1152
  118.5 6.2 %all_to_all.167 = bf16[4,2,1024]{2,1,0:T(2,128)(2,1)S(1)} all-to-all(bf16[4,2,1024]{2,1,0:T(2,128)(2,1)S(1)} %reshape.1152), channel_id=1, replica_groups=mesh['row'=128,'ch'=4] {'ch'}, dimensions={0} | all-to-all | bytes 32768 | tf_op jit(solution)/shard_map/all_to_all | solution.py:50
  124.8 0.1 reshape.1153
  125.0 0.1 all_to_all.134
  125.1 0.1 copy.96
  125.2 21.3 %all_to_all.168 = bf16[128,1,64]{2,1,0:T(2,128)(2,1)S(1)} all-to-all(bf16[128,1,64]{2,1,0:T(2,128)(2,1)S(1)} %copy.96), channel_id=1, replica_groups=mesh['row'=128,'ch'=4] {'row'}, dimensions={0} | all-to-all | bytes 32768 | tf_op jit(solution)/shard_map/all_to_all | solution.py:50
  146.6 7.6 %all_to_all.169 = bf16[4,1,128,32]{2,3,1,0:T(8,128)(2,1)S(1)} all-to-all(bf16[4,1,128,32]{2,3,1,0:T(8,128)(2,1)S(1)} %broadcast_in_dim.22), channel_id=1, replica_groups=mesh['row'=128,'ch'=4] {'ch'}, dimensions={0} | all-to-all | bytes 65536 | tf_op jit(solution)/shard_map/all_to_all | solution.py:17
  154.2 0.1 fusion.48
  154.4 21.3 %all_to_all.170 = f32[1,128,32]{2,0,1:T(1,128)S(1)} all-to-all(f32[1,128,32]{2,0,1:T(1,128)S(1)} %bitcast.238), channel_id=1, replica_groups=mesh['row'=128,'ch'=4] {'row'}, dimensions={1} | all-to-all | bytes 32768 | tf_op jit(solution)/shard_map/all_to_all | solution.py:108
  175.6 0.8 reduce.23
  176.4 0.1 reshape.1154
  176.5 7.6 %all_to_all.171 = f32[4,1,1024]{2,1,0:T(1,128)S(1)} all-to-all(f32[4,1,1024]{2,1,0:T(1,128)S(1)} %reshape.1154), channel_id=1, replica_groups=mesh['row'=128,'ch'=4] {'ch'}, dimensions={0} | all-to-all | bytes 32768 | tf_op jit(solution)/shard_map/all_to_all | solution.py:109
  184.1 0.7 reduce.24
  184.8 0.1 reshape.1155
  185.2 0.6 broadcast_in_dim.23
  185.8 3.9 %all-to-all-start.14 = ((f32[4,1,256]{2,1,0:T(1,128)}), f32[4,1,256]{2,1,0:T(1,128)S(1)}, u32[]{:S(2)}, u32[]{:S(2)}) async-start(f32[4,1,256]{2,1,0:T(1,128)} %broadcast_in_dim.23), calls=%async_computation.14 | async-start | bytes 8192 | tf_op jit(solution)/shard_map/all_to_all | solution.py:17
  189.8 0.1 all_to_all.143
  189.9 3.0 %all-to-all-done.14 = f32[4,1,256]{2,1,0:T(1,128)S(1)} async-done(((f32[4,1,256]{2,1,0:T(1,128)}), f32[4,1,256]{2,1,0:T(1,128)S(1)}, u32[]{:S(2)}, u32[]{:S(2)}) %all-to-all-start.14) | async-done | bytes 4128 | tf_op jit(solution)/shard_map/all_to_all | solution.py:17
  192.9 0.2 convolution_convert_fusion
  193.1 6.2 %all_to_all.172 = bf16[4,32,1,128]{3,1,2,0:T(8,128)(2,1)S(1)} all-to-all(bf16[4,32,1,128]{3,1,2,0:T(8,128)(2,1)S(1)} %bitcast.245), channel_id=1, replica_groups=mesh['row'=128,'ch'=4] {'ch'}, dimensions={0} | all-to-all | bytes 65536 | tf_op jit(solution)/shard_map/all_to_all | solution.py:43
  199.4 0.8 fusion.16
  (60 shorter events, 1.3 us)
Async XLA Ops:
  0.0 11.4 %copy-start = (bf16[2,128,4,32]{1,3,2,0:T(8,128)(2,1)S(1)}, bf16[2,128,4,32]{1,3,2,0:T(8,128)(2,1)}, u32[]{:S(2)}) copy-start(bf16[2,128,4,32]{1,3,2,0:T(8,128)(2,1)} %param.16) | copy-start | bytes 196612
  1.3 13.3 %all-to-all-start = ((bf16[4,32,1,128]{3,1,2,0:T(8,128)(2,1)}), bf16[4,32,1,128]{3,1,2,0:T(8,128)(2,1)S(1)}, u32[]{:S(2)}, u32[]{:S(2)}) async-start(bf16[4,32,1,128]{3,1,2,0:T(8,128)(2,1)} %broadcast_in_dim.17), calls=%async_computation | async-start | bytes 65536 | tf_op jit(solution)/shard_map/all_to_all | solution.py:17
  11.5 0.7 copy-start.4
  11.5 0.7 copy-start.9
  12.1 0.7 copy-start.3
  85.6 5.5 %copy-start.5 = (f32[2,32]{1,0:T(2,128)S(1)}, f32[2,32]{1,0:T(2,128)}, u32[]{:S(2)}) copy-start(f32[2,32]{1,0:T(2,128)} %param.20) | copy-start | bytes 772
  85.6 5.5 %copy-start.6 = (f32[2,32]{1,0:T(2,128)S(1)}, f32[2,32]{1,0:T(2,128)}, u32[]{:S(2)}) copy-start(f32[2,32]{1,0:T(2,128)} %param.19) | copy-start | bytes 772
  85.6 8.6 %all-to-all-start.5 = ((f32[4,1,1024]{2,1,0:T(1,128)}), f32[4,1,1024]{2,1,0:T(1,128)S(1)}, u32[]{:S(2)}, u32[]{:S(2)}) async-start(f32[4,1,1024]{2,1,0:T(1,128)} %reshape.1150), calls=%async_computation.5 | async-start | bytes 32768 | tf_op jit(solution)/shard_map/all_to_all | solution.py:109
  96.2 4.1 %copy-start.2 = (f32[2,32]{1,0:T(2,128)S(1)}, f32[2,32]{1,0:T(2,128)}, u32[]{:S(2)}) copy-start(f32[2,32]{1,0:T(2,128)} %param.18) | copy-start | bytes 772
  96.2 7.2 %all-to-all-start.6 = ((f32[4,1,256]{2,1,0:T(1,128)}), f32[4,1,256]{2,1,0:T(1,128)S(1)}, u32[]{:S(2)}, u32[]{:S(2)}) async-start(f32[4,1,256]{2,1,0:T(1,128)} %broadcast_in_dim.18), calls=%async_computation.6 | async-start | bytes 8192 | tf_op jit(solution)/shard_map/all_to_all | solution.py:17
  100.3 0.7 copy-start.10
  101.7 1.7 copy-start.7
  104.3 7.1 %all-to-all-start.7 = ((bf16[4,32,1,128]{3,1,2,0:T(8,128)(2,1)}), bf16[4,32,1,128]{3,1,2,0:T(8,128)(2,1)S(1)}, u32[]{:S(2)}, u32[]{:S(2)}) async-start(bf16[4,32,1,128]{3,1,2,0:T(8,128)(2,1)} %bitcast.36), calls=%async_computation.7 | async-start | bytes 65536 | tf_op jit(solution)/shard_map/all_to_all | solution.py:43
  108.9 2.5 %copy-start.1 = (bf16[32,1,128]{2,0,1:T(8,128)(2,1)S(1)}, bf16[32,1,128]{2,0,1:T(8,128)(2,1)}, u32[]{:S(2)}) copy-start(bf16[32,1,128]{2,0,1:T(8,128)(2,1)} %param.11) | copy-start | bytes 24580
  108.9 2.5 %copy-start.8 = (bf16[2,128,32]{1,2,0:T(8,128)(2,1)S(1)}, bf16[2,128,32]{1,2,0:T(8,128)(2,1)}, u32[]{:S(2)}) copy-start(bf16[2,128,32]{1,2,0:T(8,128)(2,1)} %param.17) | copy-start | bytes 49156
  185.8 7.0 %all-to-all-start.14 = ((f32[4,1,256]{2,1,0:T(1,128)}), f32[4,1,256]{2,1,0:T(1,128)S(1)}, u32[]{:S(2)}, u32[]{:S(2)}) async-start(f32[4,1,256]{2,1,0:T(1,128)} %broadcast_in_dim.23), calls=%async_computation.14 | async-start | bytes 8192 | tf_op jit(solution)/shard_map/all_to_all | solution.py:17
where the time goes:
time: 201 us; the launch traced here: 200 us
  blocking collectives  144 us (72%)
  starting transfers between devices  27.5 us (14%)
  waiting for transfers between devices  10.7 us (5%)
  local copies, waits for them, and re-layouts  9.85 us (5%)
  other arithmetic  4.72 us (2%)
  matrix products  2.92 us (1%)
    all_to_all x4, blocking collectives, sent_together(): lax.all_to_all(both, axis, split_axis=split_dim, concat_axis=concat_dim,...  66.1 us
    all_to_all x2, blocking collectives, to_rows(): lax.all_to_all(owned, 'row', split_axis=1, concat_axis=0, tiled=True)  42.5 us
    all_to_all x3, starting transfers between devices, from_everyone(): lax.all_to_all(jnp.broadcast_to(x[None], (devices, *x.shape)), axis, 0, 0...  18.1 us
    all_to_all x2, blocking collectives, from_everyone(): lax.all_to_all(jnp.broadcast_to(x[None], (devices, *x.shape)), axis, 0, 0...  13.9 us
    all_to_all x2, blocking collectives, sum_at_owner(): tiles = lax.all_to_all(in_blocks(x, dim, devices), axis, 0, 0, tiled=True)  13.9 us
    all_to_all x1, blocking collectives, to_rows(): return lax.all_to_all(blocks, 'ch', split_axis=0, concat_axis=2, tiled=True)  7.58 us
    all_to_all x1, starting transfers between devices, to_rows(): return lax.all_to_all(blocks, 'ch', split_axis=0, concat_axis=2, tiled=True)  5.46 us
    all_to_all x3, waiting for transfers between devices, from_everyone(): lax.all_to_all(jnp.broadcast_to(x[None], (devices, *x.shape)), axis, 0, 0...  5.1 us
  transfers between devices with their start and end apart: 5, of which 5 were waited for; matrix products, arithmetic and copies ran while one was open for 1% of the time, Pallas kernels for 0%

commit v1 on v0

--- a/solution.py
+++ b/solution.py
@@ -105,7 +105,10 @@
 
 
 def to_rows(owned):
-    blocks = lax.all_to_all(owned, "row", split_axis=1, concat_axis=0, tiled=True)
+    size = lax.axis_size("row")
+    shards = jnp.stack(jnp.split(owned, size, axis=1), axis=0)
+    shards = lax.all_to_all(shards, "row", split_axis=0, concat_axis=0)
+    blocks = jnp.concatenate(shards, axis=0)
     return lax.all_to_all(blocks, "ch", split_axis=0, concat_axis=2, tiled=True)
 
 

time: 201 us -> 212 us (1.055)
  local copies, waits for them, and re-layouts: 9.85 us -> 19.3 us
    split x0 -> x14, local copies, waits for them, and re-layouts: none -> 7.6 us  [to_rows(): shards = jnp.stack(jnp.split(owned, size, axis=1), axis=0)]
    unnamed x30 -> x284, local copies, waits for them, and re-layouts: 3.54 us -> 5.81 us
where the time goes in v1:
time: 212 us; the launch traced here: 211 us
  blocking collectives  144 us (68%)
  starting transfers between devices  27.5 us (13%)
  local copies, waits for them, and re-layouts  19.3 us (9%)
  waiting for transfers between devices  10.8 us (5%)
  other arithmetic  4.65 us (2%)
  matrix products  2.92 us (1%)
    all_to_all x4, blocking collectives, sent_together(): lax.all_to_all(both, axis, split_axis=split_dim, concat_axis=concat_dim,...  66.3 us
    all_to_all x2, blocking collectives, to_rows(): shards = lax.all_to_all(shards, 'row', split_axis=0, concat_axis=0)  42.5 us
    all_to_all x3, starting transfers between devices, from_everyone(): lax.all_to_all(jnp.broadcast_to(x[None], (devices, *x.shape)), axis, 0, 0...  18.1 us
    all_to_all x2, blocking collectives, from_everyone(): lax.all_to_all(jnp.broadcast_to(x[None], (devices, *x.shape)), axis, 0, 0...  13.9 us
    all_to_all x2, blocking collectives, sum_at_owner(): tiles = lax.all_to_all(in_blocks(x, dim, devices), axis, 0, 0, tiled=True)  13.9 us
    split x14, local copies, waits for them, and re-layouts, to_rows(): shards = jnp.stack(jnp.split(owned, size, axis=1), axis=0)  7.6 us
    all_to_all x1, blocking collectives, to_rows(): return lax.all_to_all(blocks, 'ch', split_axis=0, concat_axis=2, tiled=True)  7.58 us
    unnamed x284, local copies, waits for them, and re-layouts  5.81 us
  transfers between devices with their start and end apart: 5, of which 5 were waited for; matrix products, arithmetic and copies ran while one was open for 1% of the time, Pallas kernels for 0%

profile of v1, /device:TPU:1, one launch (start us, length us, event | category | flops | bytes accessed | tf_op | source)
XLA Modules:
  0.0 210.7 jit_solution(2166150122327003415)
XLA Ops:
  0.0 1.3 broadcast_in_dim.17
  1.3 10.1 %all-to-all-start = ((bf16[4,32,1,128]{3,1,2,0:T(8,128)(2,1)}), bf16[4,32,1,128]{3,1,2,0:T(8,128)(2,1)S(1)}, u32[]{:S(2)}, u32[]{:S(2)}) async-start(bf16[4,32,1,128]{3,1,2,0:T(8,128)(2,1)} %broadcast_in_dim.17), calls=%async_computation | async-start | bytes 65536 | tf_op jit(solution)/shard_map/all_to_all | solution.py:17
  11.5 0.6 copy-done.9
  12.1 0.7 copy-done.4
  12.8 0.6 dynamic_slice.7
  13.4 0.6 broadcast_multiply_fusion
  14.0 0.6 all-to-all-done
  14.7 0.2 fusion.70
  14.9 0.1 copy.854
  15.2 6.2 %all_to_all.148 = bf16[4,2,1024]{2,1,0:T(2,128)(2,1)S(1)} all-to-all(bf16[4,2,1024]{2,1,0:T(2,128)(2,1)S(1)} %reshape.1406), channel_id=1, replica_groups=mesh['row'=128,'ch'=4] {'ch'}, dimensions={0} | all-to-all | bytes 32768 | tf_op jit(solution)/shard_map/all_to_all | solution.py:50
  21.9 32.3 %all_to_all.149 = bf16[128,1,64]{2,1,0:T(2,128)(2,1)S(1)} all-to-all(bf16[128,1,64]{2,1,0:T(2,128)(2,1)S(1)} %copy.856), channel_id=1, replica_groups=mesh['row'=128,'ch'=4] {'row'}, dimensions={0} | all-to-all | bytes 32768 | tf_op jit(solution)/shard_map/all_to_all | solution.py:50
  54.3 0.2 convolution_convert_fusion.2
  54.5 7.7 %all_to_all.150 = bf16[4,1,128,32]{2,3,1,0:T(8,128)(2,1)S(1)} all-to-all(bf16[4,1,128,32]{2,3,1,0:T(8,128)(2,1)S(1)} %bitcast.771), channel_id=1, replica_groups=mesh['row'=128,'ch'=4] {'ch'}, dimensions={0} | all-to-all | bytes 65536 | tf_op jit(solution)/shard_map/all_to_all | solution.py:43
  62.2 0.4 slice_reduce_fusion.242
  62.6 0.6 slice_reduce_fusion.223
  63.2 0.6 slice_reduce_fusion.204
  63.8 0.6 slice_reduce_fusion.185
  64.3 0.6 slice_reduce_fusion.166
  64.9 0.6 slice_reduce_fusion.147
  65.4 0.6 slice_reduce_fusion.128
  67.5 21.3 %all_to_all.151 = f32[128,1,1,32]{3,2,1,0:T(1,128)S(1)} all-to-all(f32[128,1,1,32]{3,2,1,0:T(1,128)S(1)} %constant_dynamic-update-slice_fusion), channel_id=1, replica_groups=mesh['row'=128,'ch'=4] {'row'}, dimensions={0} | all-to-all | bytes 32768 | tf_op jit(solution)/shard_map/all_to_all | solution.py:110
  88.8 0.5 broadcast.803
  89.3 0.8 reduce.533
  90.1 0.7 reshape.1408
  90.8 5.5 %all-to-all-start.5 = ((f32[4,1,1024]{2,1,0:T(1,128)}), f32[4,1,1024]{2,1,0:T(1,128)S(1)}, u32[]{:S(2)}, u32[]{:S(2)}) async-start(f32[4,1,1024]{2,1,0:T(1,128)} %reshape.1408), calls=%async_computation.5 | async-start | bytes 32768 | tf_op jit(solution)/shard_map/all_to_all | solution.py:112
  96.3 3.1 %all-to-all-done.5 = f32[4,1,1024]{2,1,0:T(1,128)S(1)} async-done(((f32[4,1,1024]{2,1,0:T(1,128)}), f32[4,1,1024]{2,1,0:T(1,128)S(1)}, u32[]{:S(2)}, u32[]{:S(2)}) %all-to-all-start.5) | async-done | bytes 16416 | tf_op jit(solution)/shard_map/all_to_all | solution.py:112
  99.4 0.7 reduce.534
  100.1 0.1 reshape.1409
  100.5 0.6 broadcast_in_dim.18
  101.1 4.1 %all-to-all-start.6 = ((f32[4,1,256]{2,1,0:T(1,128)}), f32[4,1,256]{2,1,0:T(1,128)S(1)}, u32[]{:S(2)}, u32[]{:S(2)}) async-start(f32[4,1,256]{2,1,0:T(1,128)} %broadcast_in_dim.18), calls=%async_computation.6 | async-start | bytes 8192 | tf_op jit(solution)/shard_map/all_to_all | solution.py:17
  105.2 0.6 copy-done.10
  105.9 0.6 dynamic_slice.6
  106.7 1.6 all-to-all-done.6
  108.3 0.8 convolution_convert_fusion.1
  109.2 3.9 %all-to-all-start.7 = ((bf16[4,32,1,128]{3,1,2,0:T(8,128)(2,1)}), bf16[4,32,1,128]{3,1,2,0:T(8,128)(2,1)S(1)}, u32[]{:S(2)}, u32[]{:S(2)}) async-start(bf16[4,32,1,128]{3,1,2,0:T(8,128)(2,1)} %bitcast.37), calls=%async_computation.7 | async-start | bytes 65536 | tf_op jit(solution)/shard_map/all_to_all | solution.py:43
  113.1 0.6 compare_convert_fusion
  113.8 2.5 %all-to-all-done.7 = bf16[4,32,1,128]{3,1,2,0:T(8,128)(2,1)S(1)} async-done(((bf16[4,32,1,128]{3,1,2,0:T(8,128)(2,1)}), bf16[4,32,1,128]{3,1,2,0:T(8,128)(2,1)S(1)}, u32[]{:S(2)}, u32[]{:S(2)}) %all-to-all-start.7) | async-done | bytes 32800 | tf_op jit(solution)/shard_map/all_to_all | solution.py:43
  116.3 0.2 fusion.17
  116.6 6.3 %all_to_all.152 = bf16[4,32,1,128]{3,1,2,0:T(8,128)(2,1)S(1)} all-to-all(bf16[4,32,1,128]{3,1,2,0:T(8,128)(2,1)S(1)} %broadcast_in_dim.20), channel_id=1, replica_groups=mesh['row'=128,'ch'=4] {'ch'}, dimensions={0} | all-to-all | bytes 65536 | tf_op jit(solution)/shard_map/all_to_all | solution.py:17
  122.9 0.2 fusion.67
  123.2 0.1 copy.864
  123.3 0.1 reshape.1410
  123.4 6.2 %all_to_all.153 = bf16[4,2,1024]{2,1,0:T(2,128)(2,1)S(1)} all-to-all(bf16[4,2,1024]{2,1,0:T(2,128)(2,1)S(1)} %reshape.1410), channel_id=1, replica_groups=mesh['row'=128,'ch'=4] {'ch'}, dimensions={0} | all-to-all | bytes 32768 | tf_op jit(solution)/shard_map/all_to_all | solution.py:50
  130.1 21.5 %all_to_all.154 = bf16[128,1,64]{2,1,0:T(2,128)(2,1)S(1)} all-to-all(bf16[128,1,64]{2,1,0:T(2,128)(2,1)S(1)} %copy.866), channel_id=1, replica_groups=mesh['row'=128,'ch'=4] {'row'}, dimensions={0} | all-to-all | bytes 32768 | tf_op jit(solution)/shard_map/all_to_all | solution.py:50
  151.7 7.6 %all_to_all.155 = bf16[4,1,128,32]{2,3,1,0:T(8,128)(2,1)S(1)} all-to-all(bf16[4,1,128,32]{2,3,1,0:T(8,128)(2,1)S(1)} %broadcast_in_dim.22), channel_id=1, replica_groups=mesh['row'=128,'ch'=4] {'ch'}, dimensions={0} | all-to-all | bytes 65536 | tf_op jit(solution)/shard_map/all_to_all | solution.py:17
  159.3 0.1 convolution_bitcast_fusion.2
  159.4 0.5 slice_reduce_fusion.114
  159.9 0.6 slice_reduce_fusion.95
  160.5 0.6 slice_reduce_fusion.76
  161.0 0.6 slice_reduce_fusion.57
  161.6 0.6 slice_reduce_fusion.38
  162.1 0.6 slice_reduce_fusion.19
  162.7 0.6 slice_reduce_fusion
  164.8 21.3 %all_to_all.156 = f32[128,1,1,32]{3,2,1,0:T(1,128)S(1)} all-to-all(f32[128,1,1,32]{3,2,1,0:T(1,128)S(1)} %constant_dynamic-update-slice_fusion.128), channel_id=1, replica_groups=mesh['row'=128,'ch'=4] {'row'}, dimensions={0} | all-to-all | bytes 32768 | tf_op jit(solution)/shard_map/all_to_all | solution.py:110
  186.1 0.8 reduce.535
  187.0 7.6 %all_to_all.157 = f32[4,1,1024]{2,1,0:T(1,128)S(1)} all-to-all(f32[4,1,1024]{2,1,0:T(1,128)S(1)} %reshape.1412), channel_id=1, replica_groups=mesh['row'=128,'ch'=4] {'ch'}, dimensions={0} | all-to-all | bytes 32768 | tf_op jit(solution)/shard_map/all_to_all | solution.py:112
  194.6 0.7 reduce.536
  195.3 0.1 reshape.1413
  195.7 0.6 broadcast_in_dim.23
  196.3 3.9 %all-to-all-start.14 = ((f32[4,1,256]{2,1,0:T(1,128)}), f32[4,1,256]{2,1,0:T(1,128)S(1)}, u32[]{:S(2)}, u32[]{:S(2)}) async-start(f32[4,1,256]{2,1,0:T(1,128)} %broadcast_in_dim.23), calls=%async_computation.14 | async-start | bytes 8192 | tf_op jit(solution)/shard_map/all_to_all | solution.py:17
  200.4 3.0 %all-to-all-done.14 = f32[4,1,256]{2,1,0:T(1,128)S(1)} async-done(((f32[4,1,256]{2,1,0:T(1,128)}), f32[4,1,256]{2,1,0:T(1,128)S(1)}, u32[]{:S(2)}, u32[]{:S(2)}) %all-to-all-start.14) | async-done | bytes 4128 | tf_op jit(solution)/shard_map/all_to_all | solution.py:17
  203.3 0.2 convolution_convert_fusion
  203.6 6.2 %all_to_all.158 = bf16[4,32,1,128]{3,1,2,0:T(8,128)(2,1)S(1)} all-to-all(bf16[4,32,1,128]{3,1,2,0:T(8,128)(2,1)S(1)} %bitcast.770), channel_id=1, replica_groups=mesh['row'=128,'ch'=4] {'ch'}, dimensions={0} | all-to-all | bytes 65536 | tf_op jit(solution)/shard_map/all_to_all | solution.py:43
  209.8 0.8 fusion.16
  (326 shorter events, 4.5 us)
Async XLA Ops:
  0.0 11.4 %copy-start = (bf16[2,128,4,32]{1,3,2,0:T(8,128)(2,1)S(1)}, bf16[2,128,4,32]{1,3,2,0:T(8,128)(2,1)}, u32[]{:S(2)}) copy-start(bf16[2,128,4,32]{1,3,2,0:T(8,128)(2,1)} %param.16) | copy-start | bytes 196612
  1.3 13.3 %all-to-all-start = ((bf16[4,32,1,128]{3,1,2,0:T(8,128)(2,1)}), bf16[4,32,1,128]{3,1,2,0:T(8,128)(2,1)S(1)}, u32[]{:S(2)}, u32[]{:S(2)}) async-start(bf16[4,32,1,128]{3,1,2,0:T(8,128)(2,1)} %broadcast_in_dim.17), calls=%async_computation | async-start | bytes 65536 | tf_op jit(solution)/shard_map/all_to_all | solution.py:17
  11.4 0.7 copy-start.9
  12.1 0.7 copy-start.4
  12.1 0.7 copy-start.3
  90.8 5.5 %copy-start.5 = (f32[2,32]{1,0:T(2,128)S(1)}, f32[2,32]{1,0:T(2,128)}, u32[]{:S(2)}) copy-start(f32[2,32]{1,0:T(2,128)} %param.20) | copy-start | bytes 772
  90.8 5.5 %copy-start.6 = (f32[2,32]{1,0:T(2,128)S(1)}, f32[2,32]{1,0:T(2,128)}, u32[]{:S(2)}) copy-start(f32[2,32]{1,0:T(2,128)} %param.19) | copy-start | bytes 772
  90.8 8.6 %all-to-all-start.5 = ((f32[4,1,1024]{2,1,0:T(1,128)}), f32[4,1,1024]{2,1,0:T(1,128)S(1)}, u32[]{:S(2)}, u32[]{:S(2)}) async-start(f32[4,1,1024]{2,1,0:T(1,128)} %reshape.1408), calls=%async_computation.5 | async-start | bytes 32768 | tf_op jit(solution)/shard_map/all_to_all | solution.py:112
  101.1 4.1 %copy-start.2 = (f32[2,32]{1,0:T(2,128)S(1)}, f32[2,32]{1,0:T(2,128)}, u32[]{:S(2)}) copy-start(f32[2,32]{1,0:T(2,128)} %param.18) | copy-start | bytes 772
  101.1 7.2 %all-to-all-start.6 = ((f32[4,1,256]{2,1,0:T(1,128)}), f32[4,1,256]{2,1,0:T(1,128)S(1)}, u32[]{:S(2)}, u32[]{:S(2)}) async-start(f32[4,1,256]{2,1,0:T(1,128)} %broadcast_in_dim.18), calls=%async_computation.6 | async-start | bytes 8192 | tf_op jit(solution)/shard_map/all_to_all | solution.py:17
  105.2 0.7 copy-start.10
  106.6 1.8 copy-start.7
  109.2 7.1 %all-to-all-start.7 = ((bf16[4,32,1,128]{3,1,2,0:T(8,128)(2,1)}), bf16[4,32,1,128]{3,1,2,0:T(8,128)(2,1)S(1)}, u32[]{:S(2)}, u32[]{:S(2)}) async-start(bf16[4,32,1,128]{3,1,2,0:T(8,128)(2,1)} %bitcast.37), calls=%async_computation.7 | async-start | bytes 65536 | tf_op jit(solution)/shard_map/all_to_all | solution.py:43
  113.8 2.5 %copy-start.1 = (bf16[32,1,128]{2,0,1:T(8,128)(2,1)S(1)}, bf16[32,1,128]{2,0,1:T(8,128)(2,1)}, u32[]{:S(2)}) copy-start(bf16[32,1,128]{2,0,1:T(8,128)(2,1)} %param.11) | copy-start | bytes 24580
  113.8 2.5 %copy-start.8 = (bf16[2,128,32]{1,2,0:T(8,128)(2,1)S(1)}, bf16[2,128,32]{1,2,0:T(8,128)(2,1)}, u32[]{:S(2)}) copy-start(bf16[2,128,32]{1,2,0:T(8,128)(2,1)} %param.17) | copy-start | bytes 49156
  196.3 7.0 %all-to-all-start.14 = ((f32[4,1,256]{2,1,0:T(1,128)}), f32[4,1,256]{2,1,0:T(1,128)S(1)}, u32[]{:S(2)}, u32[]{:S(2)}) async-start(f32[4,1,256]{2,1,0:T(1,128)} %broadcast_in_dim.23), calls=%async_computation.14 | async-start | bytes 8192 | tf_op jit(solution)/shard_map/all_to_all | solution.py:17
